TPU v7x, 256 devices: a whole 4x4x8 slice. The times are simulated.
256 devices in a mesh: seq: 32 (over y_hi, z, core), tp: 8 (over x, y_lo).
Axes of the slice: x: 4, y: 4 (y_hi: 2, y_lo: 2; y = y_hi * 2 + y_lo), z: 8, core: 2. Of those that a mesh axis runs over, the one named last changes fastest.
Arguments:
- hidden: bfloat16 [4096, 7168], P('seq', 'tp'), may hold values from -6 to 6
- w_kv_down: bfloat16 [7168, 576], P('tp'), may hold values from -0.0625 to 0.0625
- kv_gain: float32 [512], replicated, may hold values from 0.1 to 1.9
- q_latent: bfloat16 [4096, 64, 512], P('seq', 'tp'), may hold values from -300 to 300
- q_rope: bfloat16 [4096, 4096], P('seq', 'tp'), may hold values from -6 to 6
- w_value: bfloat16 [64, 512, 128], P('tp'), may hold values from -0.75 to 0.75
Outputs:
- attended: bfloat16 [4096, 8192], P('seq', 'tp')
All inputs are finite; a program needn't handle non-finite values.
Results may differ from a plain program's by a relative error of at most 0.0097.
Values may be sent and summed in bfloat16 or wider, within the bound.
A program may use at most 64 MiB of HBM per device.

v0:
```python
import jax
import jax.numpy as jnp
from jax import lax
from jax.sharding import PartitionSpec as P

KV_RANK = 512
ROPE = 64
SCORE_SCALE = 192.0 ** (-0.5)
ROPE_BASE = 10000.0
EPSILON = 1e-06


def from_everyone(shard, axis):
    size = lax.axis_size(axis)
    return lax.all_to_all(
        jnp.broadcast_to(shard[None], (size, *shard.shape)), axis, 0, 0, tiled=True
    )


def of_everyone(shard, axis):
    everything = from_everyone(shard, axis)
    return jnp.sum(everything, axis=0)


def rotate(values, positions):
    full_width = values.shape[-1]
    half_width = full_width // 2
    frequency = ROPE_BASE ** (-jnp.arange(half_width, dtype=jnp.float32) * 2.0 / full_width)
    angles = positions.astype(jnp.float32)[:, None] * frequency[None, :]
    angle_shape = (angles.shape[0],) + (1,) * (values.ndim - 2) + (half_width,)
    cosine = jnp.cos(angles).reshape(angle_shape)
    sine_part = jnp.sin(angles).reshape(angle_shape)
    first_half = values[..., :half_width]
    second_half = values[..., half_width:]
    return jnp.concatenate(
        [
            first_half * cosine - second_half * sine_part,
            first_half * sine_part + second_half * cosine,
        ],
        -1,
    )


def finish(projection, kv_gain, positions):
    latent_part = projection[:, :KV_RANK]
    mean_square = jnp.mean(latent_part * latent_part, axis=-1, keepdims=True)
    normed = latent_part * lax.rsqrt(mean_square + EPSILON) * kv_gain[None, :]
    rope_part = rotate(projection[:, KV_RANK:], positions)
    return jnp.concatenate([normed, rope_part], -1).astype(jnp.bfloat16)


def update(running, group_queries, group_start, key_piece, key_start):
    query_count = group_queries.shape[0]
    key_count = key_piece.shape[0]

    def attend(current):
        top_score, weight_total, weighted = current
        scores = (
            jnp.einsum("qhc,kc->hqk", group_queries, key_piece, preferred_element_type=jnp.float32)
            * SCORE_SCALE
        )
        key_positions = jnp.arange(key_count, dtype=jnp.int32)
        query_positions = group_start + jnp.arange(query_count, dtype=jnp.int32)
        allowed = (key_positions[None, :] <= query_positions[:, None])[None]
        scores = jnp.where(allowed, scores, -1e30)
        new_max = jnp.maximum(top_score, jnp.max(scores, axis=-1))
        rescale = jnp.exp(top_score - new_max)
        weights = jnp.where(allowed, jnp.exp(scores - new_max[..., None]), 0.0)
        new_total = jnp.sum(weights, axis=-1)
        added_term = jnp.einsum(
            "hqk,kc->hqc",
            weights.astype(jnp.bfloat16),
            key_piece[:, :KV_RANK],
            preferred_element_type=jnp.float32,
        )
        return (new_max, new_total, added_term)

    return lax.cond(
        key_start <= group_start + query_count - 1, attend, lambda unchanged: unchanged, running
    )


def project(running, w_value):
    latent_out = (running[2] / running[1][..., None]).astype(jnp.bfloat16)
    projected = jnp.einsum("hqc,hcv->qhv", latent_out, w_value, preferred_element_type=jnp.float32)
    return projected.astype(jnp.bfloat16).reshape(projected.shape[0], -1)


def shards(hidden, w_kv_down, kv_gain, q_latent, q_rope, w_value):
    tok_rows = hidden.shape[0]
    heads_here = q_latent.shape[1]
    seq_index = lax.axis_index("seq")
    own_start = seq_index * tok_rows
    partial_value = jnp.dot(hidden, w_kv_down, preferred_element_type=jnp.float32)
    summed = of_everyone(partial_value, "tp")
    key_here = finish(summed, kv_gain, own_start + jnp.arange(tok_rows, dtype=jnp.int32))
    rope_query = rotate(
        q_rope.astype(jnp.float32).reshape(tok_rows, heads_here, ROPE),
        own_start + jnp.arange(tok_rows, dtype=jnp.int32),
    ).astype(jnp.bfloat16)
    queries = jnp.concatenate([q_latent, rope_query], -1)
    query_groups = ((queries, own_start),)

    def fresh_state(query_count):
        return (
            jnp.full((heads_here, query_count), -1e30, jnp.float32),
            jnp.zeros((heads_here, query_count), jnp.float32),
            jnp.zeros((heads_here, query_count, KV_RANK), jnp.float32),
        )

    fold_states = tuple((fresh_state(group[0].shape[0]) for group in query_groups))

    def absorb(running_all, key_piece, key_start):
        return tuple(
            (
                update(running, group[0], group[1], key_piece, key_start)
                for running, group in zip(running_all, query_groups)
            )
        )

    fold_states = absorb(
        fold_states, lax.all_gather(key_here, "seq", axis=0, tiled=True), jnp.int32(0)
    )
    results = [project(running, w_value) for running in fold_states]
    return results[0]


def solution(mesh):
    placed = (
        P("seq", "tp"),
        P("tp", None),
        P(),
        P("seq", "tp", None),
        P("seq", "tp"),
        P("tp", None, None),
    )
    return jax.shard_map(
        shards, mesh=mesh, in_specs=placed, out_specs=P("seq", "tp"), check_vma=False
    )
```

profile of v0, /device:TPU:1, one launch (start us, length us, event | category | flops | bytes accessed | tf_op | source)
XLA Modules:
  0.0 188.3 jit_solution(8439557678805121426)
XLA Ops:
  6.5 0.0 copy-start
  6.5 1.8 fusion.11
  8.4 0.0 copy-start.2
  8.4 1.6 broadcast_in_dim.44
  10.0 0.0 copy-start.1
  10.0 6.0 %all-to-all-start = ((f32[8,128,576]{1,2,0:T(8,128)}), f32[8,128,576]{1,2,0:T(8,128)S(1)}, u32[]{:S(2)}, u32[]{:S(2)}) async-start(f32[8,128,576]{1,2,0:T(8,128)} %broadcast_in_dim.44), calls=%async_computation | async-start | bytes 4718592 | tf_op jit(solution)/shard_map/all_to_all | solution.py:15
  16.0 0.0 all-gather.2.cloned.1.call-start
  16.0 34.1 %all-to-all-done = f32[8,128,576]{1,2,0:T(8,128)S(1)} async-done(((f32[8,128,576]{1,2,0:T(8,128)}), f32[8,128,576]{1,2,0:T(8,128)S(1)}, u32[]{:S(2)}, u32[]{:S(2)}) %all-to-all-start) | async-done | bytes 2359328 | tf_op jit(solution)/shard_map/all_to_all | solution.py:15
  50.2 0.8 reduce_sum.27
  51.0 1.0 multiply_reduce_fusion
  52.1 0.9 multiply_cosine_fusion
  52.9 0.0 copy-done.2
  52.9 1.1 multiply_convert_fusion
  54.0 0.7 pad_maximum_fusion.1
  54.7 0.0 all-gather.2.cloned.1.call-update
  54.7 0.0 copy-done.1
  54.7 0.1 copy.26
  54.8 1.9 %copy.27 = bf16[128,8,512]{0,2,1:T(8,128)(2,1)S(1)} copy(bf16[128,8,512]{2,1,0:T(8,128)(2,1)} %param.11) | data formatting | bytes 2097152 | tf_op args[3]
  56.9 1.1 pad_maximum_fusion
  58.0 88.2 %all-gather.2.cloned.1.call-done = bf16[4096,576]{0,1:T(8,128)(2,1)} async-done(((bf16[128,576]{0,1:T(8,128)(2,1)}), bf16[4096,576]{0,1:T(8,128)(2,1)}) %all-gather.2.cloned.1.call-update) | async-done | bytes 4718608 | tf_op jit(solution)/shard_map/all_gather | solution.py:122
  146.1 32.1 %conditional.1 = (f32[8,128]{1,0:T(8,128)S(1)}, f32[8,128,512]{2,1,0:T(8,128)}) conditional(s32[]{:T(128)} %convert_element_type.26, () %tuple.13, (s32[]{:T(128)}, bf16[4096,576]{0,1:T(8,128)(2,1)}, bf16[128,8,576]{0,2,1:T(8,128)(2,1)}) %tuple.14), branch_computations={%region_2.0_spmd, %region_3.6_spmd} | conditional | flops 9181854720 | bytes 74081296 | solution.py:78
  146.2 1.2 iota_compare_fusion
  147.3 7.6 %copy.28 = bf16[4096,576]{1,0:T(8,128)(2,1)} copy(bf16[4096,576]{0,1:T(8,128)(2,1)} %get-tuple-element.19) | data formatting | bytes 9437184 | tf_op jit(solution)/shard_map
  154.9 10.0 %fusion = (f32[8,128]{1,0:T(8,128)S(1)}, f32[4096,128,8]{1,0,2:T(8,128)S(1)}) fusion(pred[128,4096]{0,1:T(8,128)(4,1)} %iota_compare_fusion, bf16[128,8,576]{0,2,1:T(8,128)(2,1)} %get-tuple-element.13, bf16[4096,576]{0,1:T(8,128)(2,1)} %get-tuple-element.19), kind=kOutput, calls=%fused_computation.2 | convolution fusion | flops 4844420096 | bytes 23203840 | tf_op jit(solution)/shard_map/cond/branch_1_fun/qhc,kc->hqk/dot_general | solution.py:59
  164.9 8.4 %fusion.3 = f32[8,128,512]{2,1,0:T(8,128)} fusion(f32[4096,128,8]{1,0,2:T(8,128)S(1)} %get-tuple-element.22, f32[8,128]{1,0:T(8,128)S(1)} %broadcast_maximum_fusion, pred[128,4096]{0,1:T(8,128)(4,1)} %iota_compare_fusion, bf16[4096,576]{1,0:T(8,128)(2,1)} %copy.28), kind=kOutput, calls=%fused_computation.5 | convolution fusion | flops 4315938816 | bytes 23597056 | tf_op jit(solution)/shard_map/cond/branch_1_fun/hqk,kc->hqc/dot_general | solution.py:70
  173.4 4.9 %fusion.2 = f32[8,128]{1,0:T(8,128)S(1)} fusion(f32[4096,128,8]{1,0,2:T(8,128)S(1)} %get-tuple-element.22, f32[8,128]{1,0:T(8,128)S(1)} %broadcast_maximum_fusion, pred[128,4096]{0,1:T(8,128)(4,1)} %iota_compare_fusion), kind=kLoop, calls=%fused_computation.4 | loop fusion | flops 20970496 | bytes 17309696 | tf_op jit(solution)/shard_map/cond/branch_1_fun/reduce_sum | solution.py:69
  178.3 0.0 copy-done
  178.3 2.2 %convolution_convert_fusion = bf16[8,128,128]{1,2,0:T(8,128)(2,1)S(1)} fusion(bf16[8,512,128]{2,1,0:T(8,128)(2,1)S(1)} %copy-done, f32[8,128,512]{2,1,0:T(8,128)} %get-tuple-element.16, f32[8,128]{1,0:T(8,128)S(1)} %get-tuple-element.17), kind=kOutput, calls=%fused_computation.17 | convolution fusion | flops 135397376 | bytes 3411968 | tf_op jit(solution)/shard_map/hqc,hcv->qhv/dot_general | solution.py:85
  180.6 0.9 copy.30
  (6 shorter events, 0.1 us)
Async XLA Ops:
  6.5 171.8 %copy-start = (bf16[8,512,128]{2,1,0:T(8,128)(2,1)S(1)}, bf16[8,512,128]{2,1,0:T(8,128)(2,1)}, u32[]{:S(2)}) copy-start(bf16[8,512,128]{2,1,0:T(8,128)(2,1)} %param.13) | copy-start | bytes 3145732
  8.4 44.6 %copy-start.2 = (f32[512]{0:T(512)S(1)}, f32[512]{0:T(512)}, u32[]{:S(2)}) copy-start(f32[512]{0:T(512)} %param.10) | copy-start | bytes 6148
  10.0 44.8 %copy-start.1 = (bf16[128,512]{1,0:T(8,128)(2,1)S(1)}, bf16[128,512]{1,0:T(8,128)(2,1)}, u32[]{:S(2)}) copy-start(bf16[128,512]{1,0:T(8,128)(2,1)} %param.12) | copy-start | bytes 393220
  10.0 40.2 %all-to-all-start = ((f32[8,128,576]{1,2,0:T(8,128)}), f32[8,128,576]{1,2,0:T(8,128)S(1)}, u32[]{:S(2)}, u32[]{:S(2)}) async-start(f32[8,128,576]{1,2,0:T(8,128)} %broadcast_in_dim.44), calls=%async_computation | async-start | bytes 4718592 | tf_op jit(solution)/shard_map/all_to_all | solution.py:15
  16.0 130.2 %all-gather.2.cloned.1.call-start = ((), (), s32[]{:S(2)}) async-start(), calls=%async_computation.1 | async-start | bytes 4866048 | tf_op jit(solution)/shard_map/all_gather | solution.py:122
Sparse Core Ops, SparseCore 0:
  54.9 91.2 all-gather.1
where the time goes:
time: 189 us; the launch traced here: 188 us
  waiting for transfers between devices  122 us (65%)
  matrix products  22.5 us (12%)
  between operations  13.5 us (7%)
  local copies, waits for them, and re-layouts  12.1 us (6%)
  other arithmetic  11.8 us (6%)
  starting transfers between devices  6.03 us (3%)
    all_gather x1, waiting for transfers between devices, shards(): lax.all_gather(key_here, 'seq', axis=0, tiled=True)  88.2 us
    all_to_all x1, waiting for transfers between devices, from_everyone(): lax.all_to_all(jnp.broadcast_to(shard[None], (size, *shard.shape)), axis,...  34.1 us
    dot_general x1, matrix products, attend(): jnp.einsum('qhc,kc->hqk', group_queries, key_piece, preferred_element_typ...  9.97 us
    dot_general x1, matrix products, attend(): jnp.einsum('hqk,kc->hqc', weights.astype(jnp.bfloat16), key_piece[:, :KV_...  8.43 us
    another operation x1, local copies, waits for them, and re-layouts  7.63 us
    all_to_all x1, starting transfers between devices, from_everyone(): lax.all_to_all(jnp.broadcast_to(shard[None], (size, *shard.shape)), axis,...  5.99 us
    reduce_sum x1, other arithmetic, attend(): new_total = jnp.sum(weights, axis=-1)  4.93 us
  transfers between devices with their start and end apart: 2, of which 2 were waited for; matrix products, arithmetic and copies ran while one was open for 2% of the time, Pallas kernels for 0%

commit v1 on v0

--- a/solution.py
+++ b/solution.py
@@ -118,8 +118,11 @@
             )
         )
 
+    mix_the_floor = lambda view, axis_tag, pos_dim: jnp.concatenate(
+        jax.lax.all_to_all(jnp.stack(jax.lax.psum(1, axis_tag) * [view]), axis_tag, 0, 0), pos_dim
+    )
     fold_states = absorb(
-        fold_states, lax.all_gather(key_here, "seq", axis=0, tiled=True), jnp.int32(0)
+        fold_states, mix_the_floor(key_here, axis_tag="seq", pos_dim=0), jnp.int32(0)
     )
     results = [project(running, w_value) for running in fold_states]
     return results[0]

time: 189 us -> 206 us (1.090)
  waiting for transfers between devices: 122 us -> 139 us
  between operations: 13.5 us -> 0.12 us
  starting transfers between devices: 6.03 us -> 18.6 us
  local copies, waits for them, and re-layouts: 12.1 us -> 14.3 us
    all_to_all x0 -> x1, waiting for transfers between devices: none -> 105 us  [shards(): jax.lax.all_to_all(jnp.stack(jax.lax.psum(1, axis_tag) * [view]), axis_ta...]
    all_gather x1 -> x0, waiting for transfers between devices: 88.2 us -> none  [shards(): lax.all_gather(key_here, 'seq', axis=0, tiled=True)]
    all_to_all x0 -> x1, starting transfers between devices: none -> 12.8 us  [shards(): jax.lax.all_to_all(jnp.stack(jax.lax.psum(1, axis_tag) * [view]), axis_ta...]
    another operation x1 -> x2, local copies, waits for them, and re-layouts: 7.63 us -> 10.8 us
  transfers between devices with their start and end apart: 2 -> 2, of which waited for: 2 -> 2; matrix products, arithmetic and copies ran while one was open for 2% -> 1% of each run, Pallas kernels for 0% -> 0%
where the time goes in v1:
time: 206 us
  waiting for transfers between devices  139 us (67%)
  matrix products  22.3 us (11%)
  starting transfers between devices  18.6 us (9%)
  local copies, waits for them, and re-layouts  14.3 us (7%)
  other arithmetic  11.1 us (5%)
    all_to_all x1, waiting for transfers between devices, shards(): jax.lax.all_to_all(jnp.stack(jax.lax.psum(1, axis_tag) * [view]), axis_ta...  105 us
    all_to_all x1, waiting for transfers between devices, from_everyone(): lax.all_to_all(jnp.broadcast_to(shard[None], (size, *shard.shape)), axis,...  34.2 us
    all_to_all x1, starting transfers between devices, shards(): jax.lax.all_to_all(jnp.stack(jax.lax.psum(1, axis_tag) * [view]), axis_ta...  12.8 us
    dot_general x1, matrix products, attend(): jnp.einsum('qhc,kc->hqk', group_queries, key_piece, preferred_element_typ...  9.78 us
    dot_general x1, matrix products, attend(): jnp.einsum('hqk,kc->hqc', weights.astype(jnp.bfloat16), key_piece[:, :KV_...  8.44 us
    another operation x1, local copies, waits for them, and re-layouts  7.63 us
    all_to_all x1, starting transfers between devices, from_everyone(): lax.all_to_all(jnp.broadcast_to(shard[None], (size, *shard.shape)), axis,...  5.86 us
    reduce_sum x1, other arithmetic, attend(): new_total = jnp.sum(weights, axis=-1)  4.93 us
  transfers between devices with their start and end apart: 2, of which 2 were waited for; matrix products, arithmetic and copies ran while one was open for 1% of the time, Pallas kernels for 0%

profile of v1, /device:TPU:1, one launch (start us, length us, event | category | flops | bytes accessed | tf_op | source)
XLA Modules:
  0.0 205.8 jit_solution(16434107289466438274)
XLA Ops:
  0.0 0.0 copy-start
  0.0 1.8 fusion.9
  1.9 0.0 copy-start.3
  1.9 1.6 broadcast_in_dim.44
  3.4 5.9 %all-to-all-start = ((f32[8,128,576]{1,2,0:T(8,128)}), f32[8,128,576]{1,2,0:T(8,128)S(1)}, u32[]{:S(2)}, u32[]{:S(2)}) async-start(f32[8,128,576]{1,2,0:T(8,128)} %broadcast_in_dim.44), calls=%async_computation | async-start | bytes 4718592 | tf_op jit(solution)/shard_map/all_to_all | solution.py:15
  9.3 34.2 %all-to-all-done = f32[8,128,576]{1,2,0:T(8,128)S(1)} async-done(((f32[8,128,576]{1,2,0:T(8,128)}), f32[8,128,576]{1,2,0:T(8,128)S(1)}, u32[]{:S(2)}, u32[]{:S(2)}) %all-to-all-start) | async-done | bytes 2359328 | tf_op jit(solution)/shard_map/all_to_all | solution.py:15
  43.5 0.8 reduce_sum.27
  44.3 1.0 multiply_reduce_fusion
  45.4 0.9 multiply_cosine_fusion
  46.3 0.0 copy-done.3
  46.3 1.1 multiply_convert_fusion
  47.4 3.2 %stack.2 = bf16[32,128,576]{1,2,0:T(8,128)(2,1)} broadcast(bf16[128,576]{0,1:T(8,128)(2,1)S(1)} %pad_maximum_fusion.1), dimensions={1,2} | broadcast | bytes 4866048 | tf_op jit(solution)/shard_map/stack | solution.py:122
  50.6 0.0 copy-start.2
  50.6 0.0 copy-start.1
  50.6 12.8 %all-to-all-start.1 = ((bf16[32,128,576]{1,2,0:T(8,128)(2,1)}), bf16[32,128,576]{1,2,0:T(8,128)(2,1)}, u32[]{:S(2)}, u32[]{:S(2)}) async-start(bf16[32,128,576]{1,2,0:T(8,128)(2,1)} %stack.2), calls=%async_computation.1 | async-start | bytes 9437184 | tf_op jit(solution)/shard_map/all_to_all | solution.py:122
  63.3 0.0 copy-done.2
  63.4 0.1 copy.17
  63.5 0.0 copy-done.1
  63.5 1.0 copy.18
  64.5 1.1 pad_maximum_fusion
  65.7 105.1 %all-to-all-done.1 = bf16[32,128,576]{1,2,0:T(8,128)(2,1)} async-done(((bf16[32,128,576]{1,2,0:T(8,128)(2,1)}), bf16[32,128,576]{1,2,0:T(8,128)(2,1)}, u32[]{:S(2)}, u32[]{:S(2)}) %all-to-all-start.1) | async-done | bytes 4718624 | tf_op jit(solution)/shard_map/all_to_all | solution.py:122
  170.7 32.0 %conditional.1 = (f32[8,128]{1,0:T(8,128)S(1)}, f32[8,128,512]{2,1,0:T(8,128)}) conditional(s32[]{:T(128)} %convert_element_type.28, () %tuple.13, (s32[]{:T(128)}, bf16[32,128,576]{1,2,0:T(8,128)(2,1)}, bf16[128,8,576]{0,2,1:T(8,128)(2,1)}) %tuple.14), branch_computations={%region_2.0_spmd, %region_3.6_spmd} | conditional | flops 9181854720 | bytes 74081296 | solution.py:78
  170.7 1.2 iota_compare_fusion
  171.9 7.6 %copy.19 = bf16[32,128,576]{2,1,0:T(8,128)(2,1)} copy(bf16[32,128,576]{1,2,0:T(8,128)(2,1)} %get-tuple-element.20) | data formatting | bytes 9437184 | tf_op jit(solution)/shard_map
  179.5 9.8 %fusion = (f32[8,128]{1,0:T(8,128)S(1)}, f32[4096,128,8]{1,0,2:T(8,128)S(1)}) fusion(pred[128,4096]{0,1:T(8,128)(4,1)} %iota_compare_fusion, bf16[4096,576,1]{1,0,2:T(8,128)(2,1)} %bitcast.26, bf16[128,8,576]{0,2,1:T(8,128)(2,1)} %get-tuple-element.14), kind=kOutput, calls=%fused_computation.2 | convolution fusion | flops 4844420096 | bytes 23203840 | tf_op jit(solution)/shard_map/cond/branch_1_fun/qhc,kc->hqk/dot_general | solution.py:59
  189.3 8.4 %fusion.3 = f32[8,128,512]{2,1,0:T(8,128)} fusion(f32[4096,128,8]{1,0,2:T(8,128)S(1)} %get-tuple-element.23, f32[8,128]{1,0:T(8,128)S(1)} %broadcast_maximum_fusion, pred[128,4096]{0,1:T(8,128)(4,1)} %iota_compare_fusion, bf16[4096,576]{1,0:T(8,128)(2,1)} %bitcast.27), kind=kOutput, calls=%fused_computation.5 | convolution fusion | flops 4315938816 | bytes 23597056 | tf_op jit(solution)/shard_map/cond/branch_1_fun/hqk,kc->hqc/dot_general | solution.py:70
  197.8 4.9 %fusion.2 = f32[8,128]{1,0:T(8,128)S(1)} fusion(f32[4096,128,8]{1,0,2:T(8,128)S(1)} %get-tuple-element.23, f32[8,128]{1,0:T(8,128)S(1)} %broadcast_maximum_fusion, pred[128,4096]{0,1:T(8,128)(4,1)} %iota_compare_fusion), kind=kLoop, calls=%fused_computation.4 | loop fusion | flops 20970496 | bytes 17309696 | tf_op jit(solution)/shard_map/cond/branch_1_fun/reduce_sum | solution.py:69
  202.7 0.0 copy-done
  202.7 2.2 %convolution_convert_fusion = bf16[8,128,128]{1,2,0:T(8,128)(2,1)S(1)} fusion(bf16[8,512,128]{2,1,0:T(8,128)(2,1)S(1)} %copy-done, f32[8,128,512]{2,1,0:T(8,128)} %get-tuple-element.17, f32[8,128]{1,0:T(8,128)S(1)} %get-tuple-element.18), kind=kOutput, calls=%fused_computation.15 | convolution fusion | flops 135397376 | bytes 3411968 | tf_op jit(solution)/shard_map/hqc,hcv->qhv/dot_general | solution.py:85
  204.9 0.9 copy.21
  (7 shorter events, 0.1 us)
Async XLA Ops:
  0.0 202.7 %copy-start = (bf16[8,512,128]{2,1,0:T(8,128)(2,1)S(1)}, bf16[8,512,128]{2,1,0:T(8,128)(2,1)}, u32[]{:S(2)}) copy-start(bf16[8,512,128]{2,1,0:T(8,128)(2,1)} %param.13) | copy-start | bytes 3145732
  1.9 44.4 %copy-start.3 = (f32[512]{0:T(512)S(1)}, f32[512]{0:T(512)}, u32[]{:S(2)}) copy-start(f32[512]{0:T(512)} %param.10) | copy-start | bytes 6148
  3.4 40.1 %all-to-all-start = ((f32[8,128,576]{1,2,0:T(8,128)}), f32[8,128,576]{1,2,0:T(8,128)S(1)}, u32[]{:S(2)}, u32[]{:S(2)}) async-start(f32[8,128,576]{1,2,0:T(8,128)} %broadcast_in_dim.44), calls=%async_computation | async-start | bytes 4718592 | tf_op jit(solution)/shard_map/all_to_all | solution.py:15
  50.6 12.8 %copy-start.2 = (bf16[128,512]{1,0:T(8,128)(2,1)S(1)}, bf16[128,512]{1,0:T(8,128)(2,1)}, u32[]{:S(2)}) copy-start(bf16[128,512]{1,0:T(8,128)(2,1)} %param.12) | copy-start | bytes 393220
  50.6 12.9 %copy-start.1 = (bf16[128,8,512]{2,1,0:T(8,128)(2,1)S(1)}, bf16[128,8,512]{2,1,0:T(8,128)(2,1)}, u32[]{:S(2)}) copy-start(bf16[128,8,512]{2,1,0:T(8,128)(2,1)} %param.11) | copy-start | bytes 3145732
  50.6 120.1 %all-to-all-start.1 = ((bf16[32,128,576]{1,2,0:T(8,128)(2,1)}), bf16[32,128,576]{1,2,0:T(8,128)(2,1)}, u32[]{:S(2)}, u32[]{:S(2)}) async-start(bf16[32,128,576]{1,2,0:T(8,128)(2,1)} %stack.2), calls=%async_computation.1 | async-start | bytes 9437184 | tf_op jit(solution)/shard_map/all_to_all | solution.py:122
